TPU v7x, 512 devices: a whole 4x8x8 slice. The times are simulated.
512 devices in a mesh: streams: 16 (over y, core), tp: 32 (over x, z).
Axes of the slice: x: 4, y: 8, z: 8, core: 2. Of those that a mesh axis runs over, the one named last changes fastest.
Arguments:
- hidden_in: bfloat16 [512, 4, 1024], P(('streams', 'tp')), may hold values from -6 to 6
- byte_qkv: bfloat16 [512, 4, 1536], P(('streams', 'tp'))
- byte_cache: bfloat16 [512, 256, 512], P(('streams', 'tp'))
- byte_len: int32 [512], P(('streams', 'tp')), may hold values from 2 to 256, as said below
- flags: int32 [512, 4], P(('streams', 'tp')), may hold values 0 or 1
- coarse_prev: bfloat16 [512, 1024], P(('streams', 'tp')), may hold values from -6 to 6
- owner_map: int32 [32, 16, 1], replicated, may hold values from 0 to 15; in each aligned block of 16 rows (0 to 15, 16 to 31, ..., all dimensions but the last counted through in order) at most 2 rows name the same one
- up_weight: bfloat16 [1024, 8192], P(None, 'tp'), may hold values from -0.1875 to 0.1875
- coarse_gain: float32 [8192], replicated, may hold values from 0.5 to 1.5
- query_weight: bfloat16 [8192, 4096], P(None, 'tp'), may hold values from -0.0625 to 0.0625
- keyval_weight: bfloat16 [8192, 1024], P('tp'), may hold values from -0.0625 to 0.0625
- return_weight: bfloat16 [4096, 1024], P('tp'), may hold values from -0.09375 to 0.09375
- coarse_cache: bfloat16 [16, 64, 32, 32, 256], P('streams', None, 'tp'), as said below
- coarse_len: int32 [16, 64], P('streams'), may hold values from 1 to 32, as said below
Outputs:
- byte_out: bfloat16 [512, 4, 1024], P(('streams', 'tp'))
Inputs may be any that keep to these rules, and one draw needn't show every extreme that they name: `owner_map`: within one index c of tp, no group owns more than 2 of the sequences s * 32 + c, and some group owns exactly 2. `byte_len`: some sequence has exactly 256 filled positions. `coarse_len`: some slot has exactly 32 filled positions. `coarse_cache`: the copies for heads h and h2 are equal where h // 8 = h2 // 8.
All inputs are finite; a program needn't handle non-finite values. No bound on the sum of `flags` on one device may be relied on, other than what follows from the above.
Results may differ from a plain program's by a relative error of at most 0.014.
Values may be sent and summed in bfloat16 or wider, within the bound.
A program may use at most 64 MiB of HBM per device.

v0:
```python
import jax
import jax.numpy as jnp
from jax import lax
from jax.sharding import PartitionSpec as P

HD = 128
OWNED_MOST = 2
EPSILON = 1e-05
NEG_FILL = -1e30


def split_softmax(scores_old, scores_new):
    largest = jnp.maximum(
        jnp.max(scores_old, axis=-1, keepdims=True), jnp.max(scores_new, axis=-1, keepdims=True)
    )
    exp_old = jnp.exp(scores_old - largest)
    exp_new = jnp.exp(scores_new - largest)
    denominator = jnp.sum(exp_old, axis=-1, keepdims=True) + jnp.sum(
        exp_new, axis=-1, keepdims=True
    )
    return (
        (exp_old / denominator).astype(jnp.bfloat16),
        (exp_new / denominator).astype(jnp.bfloat16),
    )


def rank_table(owner_map):
    owners = owner_map[:, :, 0]
    group_total = owners.shape[1]
    same_owner = owners[:, :, None] == owners[:, None, :]
    earlier = (
        jnp.arange(group_total, dtype=jnp.int32)[None, :, None]
        > jnp.arange(group_total, dtype=jnp.int32)[None, None, :]
    )
    ranking = jnp.sum((same_owner & earlier).astype(jnp.int32), axis=2)
    return (owners, ranking)


def byte_attention(byte_qkv, byte_cache, byte_len):
    number, step_count, total_width = byte_qkv.shape
    length = byte_cache.shape[1]
    kv_width = byte_cache.shape[2] // 2
    kv_groups = kv_width // HD
    head_count = (total_width - 2 * kv_width) // HD
    group_size = head_count // kv_groups
    query_part = byte_qkv[:, :, : head_count * HD].reshape(
        number, step_count, kv_groups, group_size, HD
    )
    new_keys = byte_qkv[:, :, head_count * HD : head_count * HD + kv_width].reshape(
        number, step_count, kv_groups, HD
    )
    new_values = byte_qkv[:, :, head_count * HD + kv_width :].reshape(
        number, step_count, kv_groups, HD
    )
    old_keys = byte_cache[:, :, :kv_width].reshape(number, length, kv_groups, HD)
    old_values = byte_cache[:, :, kv_width:].reshape(number, length, kv_groups, HD)
    scaling = HD ** (-0.5)
    scores_old = (
        jnp.einsum("nsgjd,nlgd->nsgjl", query_part, old_keys, preferred_element_type=jnp.float32)
        * scaling
    )
    valid_old = jnp.arange(length, dtype=jnp.int32)[None, :] < byte_len[:, None]
    scores_old = jnp.where(valid_old[:, None, None, None, :], scores_old, NEG_FILL)
    scores_new = (
        jnp.einsum("nsgjd,nugd->nsgju", query_part, new_keys, preferred_element_type=jnp.float32)
        * scaling
    )
    causal = jnp.arange(step_count)[:, None] >= jnp.arange(step_count)[None, :]
    scores_new = jnp.where(causal[None, :, None, None, :], scores_new, NEG_FILL)
    weights_old, weights_new = split_softmax(scores_old, scores_new)
    mixed_heads = jnp.einsum(
        "nsgjl,nlgd->nsgjd", weights_old, old_values, preferred_element_type=jnp.float32
    )
    mixed_heads = mixed_heads + jnp.einsum(
        "nsgju,nugd->nsgjd", weights_new, new_values, preferred_element_type=jnp.float32
    )
    return mixed_heads.reshape(number, step_count, head_count * HD)


def dispatch(block_rows, block_marks, owners, ranking):
    column_total = lax.axis_size("tp")
    row_index = lax.axis_index("streams")
    every_rows, every_marks = (
        lax.all_gather(block_rows, ("streams", "tp"), axis=0, tiled=True),
        lax.all_gather(block_marks, ("streams", "tp"), axis=0, tiled=True),
    )
    target = jnp.where(
        owners == row_index,
        jnp.arange(column_total, dtype=jnp.int32)[:, None] * OWNED_MOST + ranking,
        -1,
    )
    target_flat = target.T.reshape(-1)
    slot_ids = jnp.arange(column_total * OWNED_MOST, dtype=jnp.int32)
    picker = (slot_ids[:, None] == target_flat[None, :]).astype(jnp.bfloat16)
    slot_rows = jnp.einsum(
        "ai,ibd->abd", picker, every_rows, preferred_element_type=jnp.float32
    ).astype(jnp.bfloat16)
    slot_marks = jnp.einsum("ai,ib->ab", picker, every_marks, preferred_element_type=jnp.float32)
    return (slot_rows, slot_marks)


def coarse_project(slot_rows, up_weight, coarse_gain, query_weight, keyval_weight):
    column_total = lax.axis_size("tp")
    column = lax.axis_index("tp")
    part_width = up_weight.shape[1]
    expanded = jnp.einsum(
        "rbd,df->rbf", slot_rows, up_weight, preferred_element_type=jnp.float32
    ).astype(jnp.bfloat16)
    widened = lax.all_gather(expanded, "tp", axis=2, tiled=True).astype(jnp.float32)
    scaled_part = (widened * coarse_gain).astype(jnp.bfloat16)
    query_sum = jnp.einsum(
        "rbf,fh->rbh", scaled_part, query_weight, preferred_element_type=jnp.float32
    )
    squares = jnp.sum(widened * widened, axis=2)
    query_sum, squares = (query_sum, squares)
    own_gains = lax.dynamic_slice_in_dim(coarse_gain, column * part_width, part_width, 0)
    own_scaled = (expanded.astype(jnp.float32) * own_gains).astype(jnp.bfloat16)
    inverse = lax.rsqrt(squares / (part_width * column_total) + EPSILON)[:, :, None]
    queries = (query_sum * inverse).astype(jnp.bfloat16)
    kv_width = keyval_weight.shape[1]
    kv_heads = kv_width // (2 * HD)
    group_size = column_total // kv_heads
    head_group = column // group_size
    keyval_part = jnp.einsum(
        "rbf,fc->rbc", own_scaled, keyval_weight, preferred_element_type=jnp.float32
    )
    keyvals = lax.psum(keyval_part, "tp")
    new_keys = (lax.dynamic_slice_in_dim(keyvals, head_group * HD, HD, 2) * inverse).astype(
        jnp.bfloat16
    )
    new_values = (
        lax.dynamic_slice_in_dim(keyvals, (kv_heads + head_group) * HD, HD, 2) * inverse
    ).astype(jnp.bfloat16)
    return (queries, new_keys, new_values)


def coarse_attention(queries, step_ids, cache_own, cache_len, key_store, value_store, mark_store):
    length = cache_own.shape[1]
    step_count = key_store.shape[1]
    scaling = HD ** (-0.5)
    scores_old = (
        jnp.einsum(
            "rbd,rld->rbl", queries, cache_own[:, :, :HD], preferred_element_type=jnp.float32
        )
        * scaling
    )
    valid_old = jnp.arange(length, dtype=jnp.int32)[None, :] < cache_len[:, None]
    scores_old = jnp.where(valid_old[:, None, :], scores_old, NEG_FILL)
    scores_new = (
        jnp.einsum("rbd,rud->rbu", queries, key_store, preferred_element_type=jnp.float32) * scaling
    )
    valid_new = (jnp.arange(step_count)[None, None, :] <= step_ids[None, :, None]) & (
        mark_store[:, None, :] > 0.5
    )
    scores_new = jnp.where(valid_new, scores_new, NEG_FILL)
    weights_old, weights_new = split_softmax(scores_old, scores_new)
    mixed_heads = jnp.einsum(
        "rbl,rld->rbd", weights_old, cache_own[:, :, HD:], preferred_element_type=jnp.float32
    )
    mixed_heads = mixed_heads + jnp.einsum(
        "rbu,rud->rbd", weights_new, value_store, preferred_element_type=jnp.float32
    )
    return mixed_heads.astype(jnp.bfloat16)


def give_back(mixed_heads, return_weight, owners, ranking):
    row_index = lax.axis_index("streams")
    column = lax.axis_index("tp")
    summed = lax.psum_scatter(
        jnp.einsum("rbh,hd->rbd", mixed_heads, return_weight, preferred_element_type=jnp.float32),
        "tp",
        scatter_dimension=0,
        tiled=True,
    ).astype(jnp.bfloat16)
    every_back = lax.all_gather(summed, "streams", axis=0, tiled=True)
    my_owner = lax.dynamic_index_in_dim(
        lax.dynamic_index_in_dim(owners, column, 0, keepdims=False), row_index, 0, keepdims=False
    )
    my_rank = lax.dynamic_index_in_dim(
        lax.dynamic_index_in_dim(ranking, column, 0, keepdims=False), row_index, 0, keepdims=False
    )
    return lax.dynamic_index_in_dim(every_back, my_owner * OWNED_MOST + my_rank, 0, keepdims=False)


def shards(
    hidden_in,
    byte_qkv,
    byte_cache,
    byte_len,
    flags,
    coarse_prev,
    owner_map,
    up_weight,
    coarse_gain,
    query_weight,
    keyval_weight,
    return_weight,
    coarse_cache,
    coarse_len,
):
    step_count = hidden_in.shape[1]
    attended = byte_attention(byte_qkv, byte_cache, byte_len)
    byte_rows = (hidden_in.astype(jnp.float32) + attended).astype(jnp.bfloat16)
    byte_marks = flags.astype(jnp.bfloat16)
    owners, ranking = rank_table(owner_map)
    cache_own = coarse_cache[0, :, 0]
    cache_len = coarse_len[0]
    slot_rows, slot_marks = dispatch(byte_rows, byte_marks, owners, ranking)
    queries, new_keys, new_values = coarse_project(
        slot_rows, up_weight, coarse_gain, query_weight, keyval_weight
    )
    step_ids = jnp.arange(step_count, dtype=jnp.int32)
    mixed_heads = coarse_attention(
        queries, step_ids, cache_own, cache_len, new_keys, new_values, slot_marks
    )
    given_back = give_back(mixed_heads, return_weight, owners, ranking)
    current = coarse_prev[0].astype(jnp.float32)
    outputs = []
    for step in range(step_count):
        current = jnp.where(flags[0, step] > 0, given_back[step].astype(jnp.float32), current)
        outputs.append(byte_rows[0, step].astype(jnp.float32) + current)
    return jnp.stack(outputs)[None].astype(jnp.bfloat16)


def solution(mesh):
    return jax.shard_map(
        shards,
        mesh=mesh,
        in_specs=(
            P(("streams", "tp"), None, None),
            P(("streams", "tp"), None, None),
            P(("streams", "tp"), None, None),
            P(("streams", "tp")),
            P(("streams", "tp"), None),
            P(("streams", "tp"), None),
            P(),
            P(None, "tp"),
            P(),
            P(None, "tp"),
            P("tp", None),
            P("tp", None),
            P("streams", None, "tp", None, None),
            P("streams", None),
        ),
        out_specs=P(("streams", "tp"), None, None),
        check_vma=False,
    )
```

profile of v0, /device:TPU:1, one launch (start us, length us, event | category | flops | bytes accessed | tf_op | source)
XLA Modules:
  0.0 587.4 jit_solution(7376833832583837293)
XLA Ops:
  6.5 0.0 copy-start.7
  6.6 0.0 copy-start.6
  6.6 0.0 copy-start.2
  6.6 1.1 fusion.96
  7.7 0.1 copy.173
  7.8 0.1 copy.172
  7.9 0.7 slice.62
  9.3 0.9 convolution_multiply_fusion.2
  10.2 0.2 fusion.98
  10.4 0.1 fusion.64
  10.5 0.1 fusion.63
  10.6 0.2 fusion.57
  10.8 0.1 fusion.66
  10.9 0.2 fusion.58
  11.1 0.9 fusion.32
  12.0 0.7 fusion.61
  12.7 0.6 copy.147
  13.3 0.0 all-gather.4.cloned.1.call-update
  13.3 0.0 all-gather.6.cloned.1.call-start
  13.4 0.9 convert_reduce_fusion
  14.3 0.7 select_bitcast_fusion
  15.0 0.1 eq.40
  15.1 122.9 %all-gather.4.cloned.1.call-done = bf16[512,4,1024]{2,1,0:T(4,128)(2,1)} async-done(((bf16[1,4,1024]{2,1,0:T(4,128)(2,1)}), bf16[512,4,1024]{2,1,0:T(4,128)(2,1)}) %all-gather.4.cloned.1.call-update) | async-done | bytes 4194320 | tf_op jit(solution)/shard_map/all_gather | solution.py:84
  138.0 5.7 fusion.14
  143.7 0.0 all-gather.6.cloned.1.call-update
  143.7 0.0 all-reduce.4.cloned.1.call-start
  143.8 1.2 fusion.100
  145.1 0.6 dynamic_slice.27
  146.9 90.5 %all-gather = bf16[512,1,4]{2,1,0:T(2,128)(2,1)S(1)} all-gather(bf16[1,1,4]{2,1,0:T(2,128)(2,1)S(1)} %convert_bitcast_fusion), channel_id=1, replica_groups=mesh['streams'=16,'tp'=32] {'streams','tp'}, dimensions={0}, use_global_device_ids=true | all-gather | bytes 4104 | tf_op jit(solution)/shard_map/all_gather | solution.py:85
  237.4 0.1 copy.150
  237.6 0.7 fusion.97
  240.8 0.1 dynamic_slice.23
  240.9 1.3 dynamic-slice.4
  242.8 0.1 convolution_compare_fusion
  243.0 0.1 iota_compare_fusion.2
  243.1 2.2 fusion.35
  245.3 0.0 all-reduce.4.cloned.1.call-update
  245.3 0.0 all-gather.6.cloned.1.call-done
  245.4 3.3 fusion.1
  248.6 0.2 copy-done.1
  248.8 1.2 fusion.23
  250.1 0.0 copy-start.3
  250.1 148.3 %all-reduce.4.cloned.1.call-done = f32[64,4,1024]{2,0,1:T(8,128)} async-done(((f32[64,4,1024]{2,0,1:T(8,128)}), f32[64,4,1024]{2,0,1:T(8,128)}) %all-reduce.4.cloned.1.call-update) | async-done | bytes 1048592 | tf_op jit(solution)/shard_map/psum | solution.py:127
  398.4 1.1 multiply_convert_fusion.2
  399.5 0.2 fusion.48
  399.7 0.1 copy.153
  399.8 0.1 fusion.95
  399.9 0.1 copy.154
  400.0 1.5 fusion.99
  401.5 0.1 copy.155
  401.6 0.2 fusion.44
  401.8 0.1 fusion.67
  401.9 0.1 copy.156
  402.0 0.1 copy.157
  402.1 0.1 divide_convert_fusion.5
  402.2 0.1 copy.158
  402.3 0.2 fusion.46
  402.5 1.4 fusion.28
  403.9 0.3 fusion.38
  404.2 0.7 copy.161
  404.9 125.0 %all-reduce.5 = bf16[64,4,1024]{2,1,0:T(4,128)(2,1)} all-reduce(f32[64,4,1024]{2,1,0:T(4,128)S(1)} %copy.161), channel_id=2, replica_groups=mesh['streams'=16,'tp'=32] {'tp'}, use_global_device_ids=true, to_apply=%region_11.12.clone | all-reduce | flops 262144 | bytes 1572864
  529.9 0.7 dynamic-slice_convert_fusion
  530.6 49.6 %all_gather.15 = bf16[32,4,1024]{2,1,0:T(4,128)(2,1)S(1)} all-gather(bf16[2,4,1024]{2,1,0:T(4,128)(2,1)S(1)} %dynamic-slice_convert_fusion), channel_id=1, replica_groups=mesh['streams'=16,'tp'=32] {'streams'}, dimensions={0}, use_global_device_ids=true | all-gather | bytes 278528 | tf_op jit(solution)/shard_map/all_gather | solution.py:175
  580.2 0.6 pad_maximum_fusion
  (27 shorter events, 0.2 us)
Async XLA Ops:
  6.5 242.1 %copy-start = (bf16[8192,128]{1,0:T(8,128)(2,1)S(1)}, bf16[8192,128]{1,0:T(8,128)(2,1)}, u32[]{:S(2)}) copy-start(bf16[8192,128]{1,0:T(8,128)(2,1)} %param.23) | copy-start | bytes 6291460
  6.5 140.4 %copy-start.4 = (s32[1,4]{1,0:T(1,128)S(1)}, s32[1,4]{1,0:T(1,128)}, u32[]{:S(2)}) copy-start(s32[1,4]{1,0:T(1,128)} %param.18) | copy-start | bytes 52
  6.5 131.5 %all-gather.4.cloned.1.call-start = ((), (), s32[]{:S(2)}) async-start(), calls=%async_computation | async-start | bytes 4202496 | tf_op jit(solution)/shard_map/all_gather | solution.py:84
  6.5 234.3 %copy-start.7 = (f32[8192]{0:T(1024)S(1)}, f32[8192]{0:T(1024)}, u32[]{:S(2)}) copy-start(f32[8192]{0:T(1024)} %param.22) | copy-start | bytes 98308
  6.6 236.4 %copy-start.6 = (s32[1,64]{1,0:T(1,128)S(1)}, s32[1,64]{1,0:T(1,128)}, u32[]{:S(2)}) copy-start(s32[1,64]{1,0:T(1,128)} %param.27) | copy-start | bytes 772
  6.6 236.5 %copy-start.2 = (bf16[256,1024]{1,0:T(8,128)(2,1)S(1)}, bf16[256,1024]{1,0:T(8,128)(2,1)}, u32[]{:S(2)}) copy-start(bf16[256,1024]{1,0:T(8,128)(2,1)} %param.24) | copy-start | bytes 1572868
  13.3 232.0 %all-gather.6.cloned.1.call-start = ((), (), s32[]{:S(2)}) async-start(), calls=%async_computation.1 | async-start | bytes 4325376 | tf_op jit(solution)/shard_map/all_gather | solution.py:109
  143.7 254.7 %all-reduce.4.cloned.1.call-start = ((), (), s32[]{:S(2)}) async-start(), calls=%async_computation.2 | async-start | bytes 2097152 | tf_op jit(solution)/shard_map/psum | solution.py:127
  245.4 3.5 copy-start.1
  250.1 153.9 %copy-start.3 = (bf16[128,1024]{1,0:T(8,128)(2,1)S(1)}, bf16[128,1024]{1,0:T(8,128)(2,1)}, u32[]{:S(2)}) copy-start(bf16[128,1024]{1,0:T(8,128)(2,1)} %param.25) | copy-start | bytes 786436
  401.5 178.7 %copy-start.5 = (bf16[1,1024]{1,0:T(2,128)(2,1)S(1)}, bf16[1,1024]{1,0:T(2,128)(2,1)}, u32[]{:S(2)}) copy-start(bf16[1,1024]{1,0:T(2,128)(2,1)} %param.19) | copy-start | bytes 6148
Sparse Core Ops, SparseCore 0:
  13.5 124.5 all-gather.3
  143.8 85.0 all-gather.5
  245.4 152.8 all-reduce.3
where the time goes:
time: 588 us; the launch traced here: 587 us
  waiting for transfers between devices  271 us (46%)
  blocking collectives  265 us (45%)
  between operations  18.6 us (3%)
  matrix products  15 us (3%)
  other arithmetic  9.66 us (2%)
  local copies, waits for them, and re-layouts  7.67 us (1%)
    psum x1, waiting for transfers between devices, coarse_project(): keyvals = lax.psum(keyval_part, 'tp')  148 us
    unnamed x1, blocking collectives  125 us
    all_gather x1, waiting for transfers between devices, dispatch(): lax.all_gather(block_rows, ('streams', 'tp'), axis=0, tiled=True)  123 us
    all_gather x1, blocking collectives, dispatch(): lax.all_gather(block_marks, ('streams', 'tp'), axis=0, tiled=True)  90.5 us
    all_gather x1, blocking collectives, give_back(): every_back = lax.all_gather(summed, 'streams', axis=0, tiled=True)  49.6 us
  transfers between devices with their start and end apart: 3, of which 2 were waited for; matrix products, arithmetic and copies ran while one was open for 2% of the time, Pallas kernels for 0%

commit v1 on v0

--- a/solution.py
+++ b/solution.py
@@ -7,6 +7,11 @@
 OWNED_MOST = 2
 EPSILON = 1e-05
 NEG_FILL = -1e30
+
+
+def add_all(x, name):
+    pieces = lax.all_gather(x, name)
+    return jnp.sum(pieces, axis=0)
 
 
 def split_softmax(scores_old, scores_new):
@@ -124,7 +129,7 @@
     keyval_part = jnp.einsum(
         "rbf,fc->rbc", own_scaled, keyval_weight, preferred_element_type=jnp.float32
     )
-    keyvals = lax.psum(keyval_part, "tp")
+    keyvals = add_all(keyval_part, "tp")
     new_keys = (lax.dynamic_slice_in_dim(keyvals, head_group * HD, HD, 2) * inverse).astype(
         jnp.bfloat16
     )

time: 588 us -> 668 us (1.14)
  waiting for transfers between devices: 271 us -> 343 us
  other arithmetic: 9.66 us -> 21.5 us
    all_gather x0 -> x1, waiting for transfers between devices: none -> 220 us  [add_all(): pieces = lax.all_gather(x, name)]
    psum x1 -> x0, waiting for transfers between devices: 148 us -> none  [coarse_project(): keyvals = lax.psum(keyval_part, 'tp')]
    reduce_sum x0 -> x1, other arithmetic: none -> 11.9 us  [add_all(): return jnp.sum(pieces, axis=0)]
where the time goes in v1:
time: 668 us
  waiting for transfers between devices  343 us (51%)
  blocking collectives  261 us (39%)
  other arithmetic  21.5 us (3%)
  between operations  18.6 us (3%)
  matrix products  15.4 us (2%)
  local copies, waits for them, and re-layouts  8.17 us (1%)
    all_gather x1, waiting for transfers between devices, add_all(): pieces = lax.all_gather(x, name)  220 us
    unnamed x1, blocking collectives  123 us
    all_gather x1, waiting for transfers between devices, dispatch(): lax.all_gather(block_rows, ('streams', 'tp'), axis=0, tiled=True)  123 us
    all_gather x1, blocking collectives, dispatch(): lax.all_gather(block_marks, ('streams', 'tp'), axis=0, tiled=True)  91.3 us
    all_gather x1, blocking collectives, give_back(): every_back = lax.all_gather(summed, 'streams', axis=0, tiled=True)  45.8 us
  transfers between devices with their start and end apart: 3, of which 2 were waited for; matrix products, arithmetic and copies ran while one was open for 2% of the time, Pallas kernels for 0%

profile of v1, /device:TPU:1, one launch (start us, length us, event | category | flops | bytes accessed | tf_op | source)
XLA Modules:
  0.0 667.7 jit_solution(615386057321906401)
XLA Ops:
  6.5 0.0 copy-start
  6.6 0.9 slice.62
  7.4 0.9 convolution_multiply_fusion.2
  8.3 1.0 fusion.96
  9.3 0.1 copy.172
  10.1 0.1 fusion.64
  10.1 0.2 fusion.98
  10.4 0.1 fusion.63
  10.5 0.2 fusion.57
  10.7 0.1 fusion.66
  10.8 0.1 copy.173
  10.9 0.2 fusion.58
  11.1 0.9 fusion.32
  12.0 0.7 fusion.61
  12.7 0.6 copy.147
  13.3 0.0 all-gather.6.cloned.1.call-update
  13.3 0.0 all-gather.8.cloned.1.call-start
  13.4 0.9 convert_reduce_fusion
  14.3 0.7 select_bitcast_fusion
  15.0 0.1 eq.40
  15.1 122.9 %all-gather.6.cloned.1.call-done = bf16[512,4,1024]{2,1,0:T(4,128)(2,1)} async-done(((bf16[1,4,1024]{2,1,0:T(4,128)(2,1)}), bf16[512,4,1024]{2,1,0:T(4,128)(2,1)}) %all-gather.6.cloned.1.call-update) | async-done | bytes 4194320 | tf_op jit(solution)/shard_map/all_gather | solution.py:89
  138.0 5.7 fusion.14
  143.7 0.0 all-gather.8.cloned.1.call-update
  143.7 0.0 all-gather.10.cloned.1.call-start
  143.8 0.1 dynamic_slice.23
  143.8 2.2 fusion.35
  146.0 0.0 all-gather.10.cloned.1.call-update
  146.1 0.7 dynamic_slice.27
  146.7 1.2 fusion.100
  149.3 91.3 %all-gather.1 = bf16[512,1,4]{2,1,0:T(2,128)(2,1)S(1)} all-gather(bf16[1,1,4]{2,1,0:T(2,128)(2,1)S(1)} %convert_bitcast_fusion), channel_id=1, replica_groups=mesh['streams'=16,'tp'=32] {'streams','tp'}, dimensions={0}, use_global_device_ids=true | all-gather | bytes 4104 | tf_op jit(solution)/shard_map/all_gather | solution.py:90
  240.6 0.1 copy.150
  240.7 0.7 fusion.97
  244.0 1.3 dynamic-slice.4
  245.9 0.1 convolution_compare_fusion
  246.0 0.1 iota_compare_fusion.2
  246.1 0.0 all-gather.8.cloned.1.call-done
  246.2 3.3 fusion.1
  249.5 0.6 copy-done.1
  250.1 1.2 fusion.23
  251.4 1.0 fusion.99
  252.4 220.4 %all-gather.10.cloned.1.call-done = f32[2048,4,1024]{2,0,1:T(8,128)} async-done(((f32[64,4,1024]{2,0,1:T(8,128)}), f32[2048,4,1024]{2,0,1:T(8,128)}) %all-gather.10.cloned.1.call-update) | async-done | bytes 33554448 | tf_op jit(solution)/shard_map/all_gather | solution.py:13
  472.9 11.9 %reduce_sum.67 = f32[64,4,1024]{2,0,1:T(8,128)S(1)} reduce(f32[32,64,4,1024]{3,1,0,2:T(8,128)} %bitcast.185, f32[]{:T(128)} %constant.89.clone.1), dimensions={0}, to_apply=%region_7.8 | reduce | flops 8126464 | bytes 34603012 | tf_op jit(solution)/shard_map/reduce_sum | solution.py:14
  484.7 0.1 multiply_convert_fusion.2
  484.8 1.0 fusion.48
  485.9 0.0 copy-start.5
  485.9 0.1 copy.153
  486.0 0.1 fusion.95
  486.1 0.1 copy.154
  486.2 0.1 copy.155
  486.3 0.1 fusion.67
  486.4 0.1 copy.156
  486.5 1.1 fusion.44
  487.6 0.1 copy.157
  487.7 0.1 divide_convert_fusion.5
  487.8 0.1 copy.158
  488.0 0.2 fusion.46
  488.2 1.5 fusion.28
  489.6 0.0 copy-done.3
  489.6 0.3 fusion.38
  489.9 0.7 copy.161
  490.6 123.4 %all-reduce.2 = bf16[64,4,1024]{2,1,0:T(4,128)(2,1)} all-reduce(f32[64,4,1024]{2,1,0:T(4,128)S(1)} %copy.161), channel_id=3, replica_groups=mesh['streams'=16,'tp'=32] {'tp'}, use_global_device_ids=true, to_apply=%region_11.12.clone | all-reduce | flops 262144 | bytes 1572864
  614.0 0.7 dynamic-slice_convert_fusion
  614.7 45.8 %all_gather.23 = bf16[32,4,1024]{2,1,0:T(4,128)(2,1)S(1)} all-gather(bf16[2,4,1024]{2,1,0:T(4,128)(2,1)S(1)} %dynamic-slice_convert_fusion), channel_id=1, replica_groups=mesh['streams'=16,'tp'=32] {'streams'}, dimensions={0}, use_global_device_ids=true | all-gather | bytes 278528 | tf_op jit(solution)/shard_map/all_gather | solution.py:180
  660.6 0.6 pad_maximum_fusion
  (32 shorter events, 0.2 us)
Async XLA Ops:
  6.5 243.0 %copy-start = (bf16[8192,128]{1,0:T(8,128)(2,1)S(1)}, bf16[8192,128]{1,0:T(8,128)(2,1)}, u32[]{:S(2)}) copy-start(bf16[8192,128]{1,0:T(8,128)(2,1)} %param.23) | copy-start | bytes 6291460
  6.5 137.2 %copy-start.7 = (f32[8192]{0:T(1024)S(1)}, f32[8192]{0:T(1024)}, u32[]{:S(2)}) copy-start(f32[8192]{0:T(1024)} %param.22) | copy-start | bytes 98308
  6.5 137.3 %copy-start.2 = (bf16[256,1024]{1,0:T(8,128)(2,1)S(1)}, bf16[256,1024]{1,0:T(8,128)(2,1)}, u32[]{:S(2)}) copy-start(bf16[256,1024]{1,0:T(8,128)(2,1)} %param.24) | copy-start | bytes 1572868
  6.5 131.5 %all-gather.6.cloned.1.call-start = ((), (), s32[]{:S(2)}) async-start(), calls=%async_computation | async-start | bytes 4202496 | tf_op jit(solution)/shard_map/all_gather | solution.py:89
  13.3 232.8 %all-gather.8.cloned.1.call-start = ((), (), s32[]{:S(2)}) async-start(), calls=%async_computation.1 | async-start | bytes 4325376 | tf_op jit(solution)/shard_map/all_gather | solution.py:114
  15.1 134.2 %copy-start.4 = (s32[1,4]{1,0:T(1,128)S(1)}, s32[1,4]{1,0:T(1,128)}, u32[]{:S(2)}) copy-start(s32[1,4]{1,0:T(1,128)} %param.18) | copy-start | bytes 52
  15.1 231.0 %copy-start.6 = (s32[1,64]{1,0:T(1,128)S(1)}, s32[1,64]{1,0:T(1,128)}, u32[]{:S(2)}) copy-start(s32[1,64]{1,0:T(1,128)} %param.27) | copy-start | bytes 772
  143.7 329.2 %all-gather.10.cloned.1.call-start = ((), (), s32[]{:S(2)}) async-start(), calls=%async_computation.2 | async-start | bytes 34603008 | tf_op jit(solution)/shard_map/all_gather | solution.py:13
  246.1 3.9 copy-start.1
  249.5 1.9 copy-start.8
  251.3 221.5 %copy-start.9 = (bf16[64,4,128]{2,0,1:T(8,128)(2,1)}, bf16[64,4,128]{2,0,1:T(8,128)(2,1)S(1)}, u32[]{:S(2)}) copy-start(bf16[64,4,128]{2,0,1:T(8,128)(2,1)S(1)} %fusion.23) | copy-start | bytes 196612
  472.9 16.8 %copy-start.3 = (bf16[128,1024]{1,0:T(8,128)(2,1)S(1)}, bf16[128,1024]{1,0:T(8,128)(2,1)}, u32[]{:S(2)}) copy-start(bf16[128,1024]{1,0:T(8,128)(2,1)} %param.25) | copy-start | bytes 786436
  485.9 174.6 %copy-start.5 = (bf16[1,1024]{1,0:T(2,128)(2,1)S(1)}, bf16[1,1024]{1,0:T(2,128)(2,1)}, u32[]{:S(2)}) copy-start(bf16[1,1024]{1,0:T(2,128)(2,1)} %param.19) | copy-start | bytes 6148
Sparse Core Ops, SparseCore 0:
  13.4 124.5 all-gather.5
  143.8 83.1 all-gather.7
  230.2 242.6 all-gather.9
